TPU v7x, 256 devices: a whole 4x4x8 slice. The times are simulated.
256 devices in a mesh: blk: 64 (over z, y, core), col: 4 (over x).
Axes of the slice: x: 4, y: 4, z: 8, core: 2. Of those that a mesh axis runs over, the one named last changes fastest.
Arguments:
- y_start: float32 [128, 131072], P('col', 'blk')
- tile_real: bfloat16 [6144, 256, 256], P('blk'), may hold values from 0 to 1, as said below
- tile_imag: bfloat16 [6144, 256, 256], P('blk'), may hold values from -1 to 1, as said below
- tile_rows: int32 [6144], P('blk'), may hold values from 0 to 7
- tile_slots: int32 [6144], P('blk'), may hold values from 0 to 71, as said below
- fetch_pick: int32 [64, 64], P('blk'), may hold values from 0 to 7
Outputs:
- encodings: float32 [128, 131072], P('col', 'blk')
Inputs may be any that keep to these rules, and one draw needn't show every extreme that they name: `tile_slots`: on each device the first 16 of its 96 tiles name an own row block (0 to 7); the others name 8 + p for an owning device p other than itself; every device reads from the devices 1, 32 and -1 places away along blk, modulo the axis. `tile_real`: entries are 0 or 1. `tile_imag`: entries are -1, 0 or 1, and never nonzero where tile_real is nonzero.
All inputs are finite; a program needn't handle non-finite values.
Results may differ from a plain program's by a relative error of at most 0.0031.
Values may be sent and summed in bfloat16 or wider, within the bound.
A program may use at most 128 MiB of HBM per device.

v0:
```python
import math
import jax
import jax.numpy as jnp
from jax import lax
from jax.sharding import PartitionSpec as P

LOC_RB = 2
STEPS = 4
center = 1.25
half_width = 0.75


def turn(values):
    pairs = values.reshape((values.shape[0] // 2, 2) + values.shape[1:])
    return jnp.stack([-pairs[:, 1], pairs[:, 0]], axis=1).reshape(values.shape)


def tile_products(picked, real_part, imag_part, member):
    prod_re = jnp.einsum("ctb,tab->cta", picked, real_part, preferred_element_type=jnp.float32)
    prod_im = jnp.einsum("ctb,tab->cta", picked, imag_part, preferred_element_type=jnp.float32)
    sum_re = jnp.einsum("cta,tr->cra", prod_re, member, precision=lax.Precision.HIGHEST)
    sum_im = jnp.einsum("cta,tr->cra", prod_im, member, precision=lax.Precision.HIGHEST)
    return (sum_re, sum_im)


def per_device(y_start, tile_real, tile_imag, tile_rows, tile_slots, fetch_pick):
    group, rows = y_start.shape
    order = tile_real.shape[1]
    rb_dev = rows // order
    local_count = LOC_RB * rb_dev
    nblk = lax.axis_size("blk")
    member = (tile_rows[:, None] == jnp.arange(rb_dev, dtype=jnp.int32)[None, :]).astype(
        jnp.float32
    )
    present = jnp.abs(tile_real) + jnp.abs(tile_imag)
    counted = jnp.einsum(
        "tab,b->ta", present, jnp.ones((order,), jnp.bfloat16), preferred_element_type=jnp.float32
    )
    degree = jnp.dot(member.T, counted, precision=lax.Precision.HIGHEST)
    scale = (1.0 / jnp.sqrt(jnp.maximum(degree, 1.0))).reshape(rows)
    own_slots = tile_slots[:local_count]
    owners = tile_slots[local_count:] - rb_dev
    fetch_row = fetch_pick[0]
    real_near, imag_near, member_near = (
        tile_real[:local_count],
        tile_imag[:local_count],
        member[:local_count],
    )
    real_far, imag_far, member_far = (
        tile_real[local_count:],
        tile_imag[local_count:],
        member[local_count:],
    )
    wanted = lax.all_to_all(fetch_row, "blk", split_axis=0, concat_axis=0, tiled=True)

    def operate(field):
        sent = (field * scale[None, :]).astype(jnp.bfloat16).reshape(group, rb_dev, order)
        near = jnp.take(sent, own_slots, axis=1)
        near_re, near_im = tile_products(near, real_near, imag_near, member_near)
        packed = jnp.take(sent, wanted, axis=1)
        arrived = lax.all_to_all(packed, "blk", split_axis=1, concat_axis=1, tiled=True)
        far = jnp.take(arrived, owners, axis=1)
        far_re, far_im = tile_products(far, real_far, imag_far, member_far)
        applied = (near_re + far_re + turn(near_im + far_im)).reshape(group, rows) * scale[None, :]
        return ((1.0 - center) * field - applied) / half_width

    previous = y_start
    current = operate(y_start)
    for step in range(1, STEPS):
        following = 2.0 * operate(current) - previous
        previous, current = (current, following)
    gathered = lax.all_gather(current, "col", axis=0, tiled=True)
    partial_gram = jnp.dot(gathered, gathered.T, precision=lax.Precision.HIGHEST)
    gram = lax.psum(partial_gram, "blk")
    gram = gram + turn(turn(gram).T).T
    lower = jnp.linalg.cholesky(gram)
    solved = jax.scipy.linalg.solve_triangular(lower, gathered, lower=True)
    mine = lax.dynamic_slice_in_dim(solved, lax.axis_index("col") * group, group, 0)
    return mine * math.sqrt(rows * nblk)


def solution(mesh):
    return jax.shard_map(
        per_device,
        mesh=mesh,
        in_specs=(
            P("col", "blk"),
            P("blk", None, None),
            P("blk", None, None),
            P("blk"),
            P("blk"),
            P("blk", None),
        ),
        out_specs=P("col", "blk"),
        check_vma=False,
    )
```

profile of v0, /device:TPU:1, one launch (start us, length us, event | category | flops | bytes accessed | tf_op | source)
XLA Modules:
  0.0 487.0 jit_solution(1898330010088756384)
XLA Ops:
  6.5 1.4 copy.73
  7.9 13.2 %all-to-all-start = ((s32[64,1,1]{2,1,0:T(1,128)}), s32[64,1,1]{2,1,0:T(1,128)S(1)}, u32[]{:S(2)}, u32[]{:S(2)}) async-start(s32[64,1,1]{2,1,0:T(1,128)} %copy.73), calls=%async_computation | async-start | bytes 65536 | tf_op jit(solution)/shard_map/all_to_all | solution.py:54
  21.1 10.0 %fusion = f32[1,96,256]{2,0,1:T(1,128)S(1)} fusion(bf16[96,256,256]{2,1,0:T(8,128)(2,1)} %param.14, bf16[96,256,256]{2,1,0:T(8,128)(2,1)} %param.13), kind=kOutput, calls=%fused_computation.12 | convolution fusion | flops 31457280 | bytes 25264128 | tf_op jit(solution)/shard_map/tab,b->ta/dot_general | solution.py:36
  31.3 1.2 reduce.6
  32.6 0.6 gather_fusion.1
  33.2 1.1 select_bitcast_fusion.3
  34.4 10.6 %all-to-all-start.1 = ((bf16[32,64,256]{2,0,1:T(8,128)(2,1)}), bf16[32,64,256]{2,0,1:T(8,128)(2,1)S(1)}, u32[]{:S(2)}, u32[]{:S(2)}) async-start(bf16[32,64,256]{2,0,1:T(8,128)(2,1)} %select_bitcast_fusion.3), calls=%async_computation.1 | async-start | bytes 2097152 | tf_op jit(solution)/shard_map/all_to_all | solution.py:61
  45.7 2.3 fusion.96
  48.0 3.1 fusion.84
  51.2 21.7 %all-to-all-done.1 = bf16[32,64,256]{2,0,1:T(8,128)(2,1)S(1)} async-done(((bf16[32,64,256]{2,0,1:T(8,128)(2,1)}), bf16[32,64,256]{2,0,1:T(8,128)(2,1)S(1)}, u32[]{:S(2)}, u32[]{:S(2)}) %all-to-all-start.1) | async-done | bytes 1048608 | tf_op jit(solution)/shard_map/all_to_all | solution.py:61
  72.8 0.7 gather_fusion.2
  73.5 5.7 %fusion.48 = f32[32,80,256]{2,0,1:T(8,128)S(1)} fusion(bf16[96,256,256]{2,1,0:T(8,128)(2,1)} %param.14, bf16[80,32,256]{2,1,0:T(8,128)(2,1)S(1)} %gather_fusion.2, pred[80]{0:T(512)(128)(4,1)S(1)} %get-tuple-element.10), kind=kOutput, calls=%fused_computation.52 | convolution fusion | flops 336199680 | bytes 14418000 | tf_op jit(solution)/shard_map/ctb,tab->cta/dot_general | solution.py:20
  79.2 5.7 %fusion.36 = f32[32,80,256]{2,0,1:T(8,128)S(1)} fusion(bf16[96,256,256]{2,1,0:T(8,128)(2,1)} %param.13, bf16[80,32,256]{2,1,0:T(8,128)(2,1)S(1)} %gather_fusion.2, pred[80]{0:T(512)(128)(4,1)S(1)} %get-tuple-element.10), kind=kOutput, calls=%fused_computation.48 | convolution fusion | flops 336199680 | bytes 14418000 | tf_op jit(solution)/shard_map/ctb,tab->cta/dot_general | solution.py:19
  85.0 2.4 fusion.32
  88.1 2.4 fusion.34
  90.5 0.6 fusion.115
  91.3 0.6 gather_fusion.4
  91.9 1.1 select_bitcast_fusion.2
  93.1 6.8 %all-to-all-start.2 = ((bf16[32,64,256]{2,0,1:T(8,128)(2,1)}), bf16[32,64,256]{2,0,1:T(8,128)(2,1)S(1)}, u32[]{:S(2)}, u32[]{:S(2)}) async-start(bf16[32,64,256]{2,0,1:T(8,128)(2,1)} %select_bitcast_fusion.2), calls=%async_computation.2 | async-start | bytes 2097152 | tf_op jit(solution)/shard_map/all_to_all | solution.py:61
  100.5 2.3 fusion.99
  102.8 3.1 fusion.87
  105.9 21.8 %all-to-all-done.2 = bf16[32,64,256]{2,0,1:T(8,128)(2,1)S(1)} async-done(((bf16[32,64,256]{2,0,1:T(8,128)(2,1)}), bf16[32,64,256]{2,0,1:T(8,128)(2,1)S(1)}, u32[]{:S(2)}, u32[]{:S(2)}) %all-to-all-start.2) | async-done | bytes 1048608 | tf_op jit(solution)/shard_map/all_to_all | solution.py:61
  127.8 0.8 gather_fusion.5
  128.6 5.7 %fusion.51 = f32[32,80,256]{2,0,1:T(8,128)S(1)} fusion(bf16[96,256,256]{2,1,0:T(8,128)(2,1)} %param.14, bf16[80,32,256]{2,1,0:T(8,128)(2,1)S(1)} %gather_fusion.5, pred[80]{0:T(512)(128)(4,1)S(1)} %get-tuple-element.10), kind=kOutput, calls=%fused_computation.53 | convolution fusion | flops 336199680 | bytes 14418000 | tf_op jit(solution)/shard_map/ctb,tab->cta/dot_general | solution.py:20
  134.3 5.7 %fusion.39 = f32[32,80,256]{2,0,1:T(8,128)S(1)} fusion(bf16[96,256,256]{2,1,0:T(8,128)(2,1)} %param.13, bf16[80,32,256]{2,1,0:T(8,128)(2,1)S(1)} %gather_fusion.5, pred[80]{0:T(512)(128)(4,1)S(1)} %get-tuple-element.10), kind=kOutput, calls=%fused_computation.49 | convolution fusion | flops 336199680 | bytes 14418000 | tf_op jit(solution)/shard_map/ctb,tab->cta/dot_general | solution.py:19
  140.0 2.4 fusion.28
  143.1 2.4 fusion.30
  145.6 0.6 fusion.113
  146.4 0.7 gather_fusion.7
  147.1 1.1 select_bitcast_fusion.1
  148.3 7.0 %all-to-all-start.3 = ((bf16[32,64,256]{2,0,1:T(8,128)(2,1)}), bf16[32,64,256]{2,0,1:T(8,128)(2,1)S(1)}, u32[]{:S(2)}, u32[]{:S(2)}) async-start(bf16[32,64,256]{2,0,1:T(8,128)(2,1)} %select_bitcast_fusion.1), calls=%async_computation.3 | async-start | bytes 2097152 | tf_op jit(solution)/shard_map/all_to_all | solution.py:61
  155.3 0.7 gather_fusion.6
  156.0 3.1 fusion.102
  159.1 3.1 fusion.90
  162.2 20.9 %all-to-all-done.3 = bf16[32,64,256]{2,0,1:T(8,128)(2,1)S(1)} async-done(((bf16[32,64,256]{2,0,1:T(8,128)(2,1)}), bf16[32,64,256]{2,0,1:T(8,128)(2,1)S(1)}, u32[]{:S(2)}, u32[]{:S(2)}) %all-to-all-start.3) | async-done | bytes 1048608 | tf_op jit(solution)/shard_map/all_to_all | solution.py:61
  183.1 0.8 gather_fusion.8
  183.9 5.7 %fusion.54 = f32[32,80,256]{2,0,1:T(8,128)S(1)} fusion(bf16[96,256,256]{2,1,0:T(8,128)(2,1)} %param.14, bf16[80,32,256]{2,1,0:T(8,128)(2,1)S(1)} %gather_fusion.8, pred[80]{0:T(512)(128)(4,1)S(1)} %get-tuple-element.10), kind=kOutput, calls=%fused_computation.54 | convolution fusion | flops 336199680 | bytes 14418000 | tf_op jit(solution)/shard_map/ctb,tab->cta/dot_general | solution.py:20
  189.7 5.7 %fusion.42 = f32[32,80,256]{2,0,1:T(8,128)S(1)} fusion(bf16[96,256,256]{2,1,0:T(8,128)(2,1)} %param.13, bf16[80,32,256]{2,1,0:T(8,128)(2,1)S(1)} %gather_fusion.8, pred[80]{0:T(512)(128)(4,1)S(1)} %get-tuple-element.10), kind=kOutput, calls=%fused_computation.50 | convolution fusion | flops 336199680 | bytes 14418000 | tf_op jit(solution)/shard_map/ctb,tab->cta/dot_general | solution.py:19
  195.4 2.4 fusion.24
  198.5 2.4 fusion.26
  201.8 0.7 gather_fusion.10
  202.6 1.1 select_bitcast_fusion
  203.7 6.5 %all-to-all-start.4 = ((bf16[32,64,256]{2,0,1:T(8,128)(2,1)}), bf16[32,64,256]{2,0,1:T(8,128)(2,1)S(1)}, u32[]{:S(2)}, u32[]{:S(2)}) async-start(bf16[32,64,256]{2,0,1:T(8,128)(2,1)} %select_bitcast_fusion), calls=%async_computation.4 | async-start | bytes 2097152 | tf_op jit(solution)/shard_map/all_to_all | solution.py:61
  210.4 0.7 gather_fusion.9
  211.1 3.1 fusion.105
  214.3 3.1 fusion.93
  217.4 20.8 %all-to-all-done.4 = bf16[32,64,256]{2,0,1:T(8,128)(2,1)S(1)} async-done(((bf16[32,64,256]{2,0,1:T(8,128)(2,1)}), bf16[32,64,256]{2,0,1:T(8,128)(2,1)S(1)}, u32[]{:S(2)}, u32[]{:S(2)}) %all-to-all-start.4) | async-done | bytes 1048608 | tf_op jit(solution)/shard_map/all_to_all | solution.py:61
  238.2 0.8 gather_fusion.11
  239.0 5.7 %fusion.57 = f32[32,80,256]{2,0,1:T(8,128)S(1)} fusion(bf16[96,256,256]{2,1,0:T(8,128)(2,1)} %param.14, bf16[80,32,256]{2,1,0:T(8,128)(2,1)S(1)} %gather_fusion.11, pred[80]{0:T(512)(128)(4,1)S(1)} %get-tuple-element.10), kind=kOutput, calls=%fused_computation.55 | convolution fusion | flops 336199680 | bytes 14418000 | tf_op jit(solution)/shard_map/ctb,tab->cta/dot_general | solution.py:20
  244.7 5.7 %fusion.45 = f32[32,80,256]{2,0,1:T(8,128)S(1)} fusion(bf16[96,256,256]{2,1,0:T(8,128)(2,1)} %param.13, bf16[80,32,256]{2,1,0:T(8,128)(2,1)S(1)} %gather_fusion.11, pred[80]{0:T(512)(128)(4,1)S(1)} %get-tuple-element.10), kind=kOutput, calls=%fused_computation.51 | convolution fusion | flops 336199680 | bytes 14418000 | tf_op jit(solution)/shard_map/ctb,tab->cta/dot_general | solution.py:19
  250.5 2.4 fusion.20
  253.6 2.4 fusion.22
  256.7 0.9 multiply_subtract_fusion
  257.9 22.6 %all-gather.2.cloned.1.call-done = f32[128,2048]{1,0:T(8,128)} async-done(((f32[32,2048]{1,0:T(8,128)}), f32[128,2048]{1,0:T(8,128)}) %all-gather.2.cloned.1.call-update) | async-done | bytes 1048592 | tf_op jit(solution)/shard_map/all_gather | solution.py:72
  280.5 3.3 fusion.190
  283.8 169.2 %all-reduce.2.cloned.1.call-done = f32[128,128]{0,1:T(8,128)} async-done(((f32[128,128]{0,1:T(8,128)}), f32[128,128]{0,1:T(8,128)}) %all-reduce.2.cloned.1.call-update) | async-done | bytes 65552 | tf_op jit(solution)/shard_map/psum | solution.py:74
  453.0 0.9 copy.97
  454.3 0.8 add.120
  455.3 11.7 %cholesky.16 = f32[128,128]{1,0:T(8,128)S(1)} custom-call(f32[128,128]{1,0:T(8,128)S(1)} %fusion.139), custom_call_target="Cholesky" | custom-call | tf_op jit(solution)/shard_map/jit(cholesky)/cholesky | solution.py:76
  467.0 0.6 compare_reduce_fusion
  467.7 0.7 fusion.136
  468.3 9.8 %custom-call.7 = f32[1,128,128]{1,2,0:T(8,128)S(1)} custom-call(f32[1,128,128]{2,1,0:T(8,128)S(1)} %fusion.136), custom_call_target="InvertDiagBlocksLowerTriangular" | custom-call | tf_op jit(solution)/shard_map/jit(_solve_triangular)/triangular_solve | solution.py:77
  478.2 1.1 fusion.137
  479.2 0.7 dynamic-slice_multiply_fusion
  (92 shorter events, 6.9 us)
Async XLA Ops:
  7.9 23.4 %all-to-all-start = ((s32[64,1,1]{2,1,0:T(1,128)}), s32[64,1,1]{2,1,0:T(1,128)S(1)}, u32[]{:S(2)}, u32[]{:S(2)}) async-start(s32[64,1,1]{2,1,0:T(1,128)} %copy.73), calls=%async_computation | async-start | bytes 65536 | tf_op jit(solution)/shard_map/all_to_all | solution.py:54
  21.1 10.0 %copy-start.18 = (s32[96]{0:T(128)S(1)}, s32[96]{0:T(128)}, u32[]{:S(2)}) copy-start(s32[96]{0:T(128)} %param.15) | copy-start | bytes 1156
  21.1 10.2 %copy-start.1 = (f32[32,2048]{1,0:T(8,128)S(1)}, f32[32,2048]{1,0:T(8,128)}, u32[]{:S(2)}) copy-start(f32[32,2048]{1,0:T(8,128)} %param.12) | copy-start | bytes 786436
  32.6 59.4 %copy-start.15 = (pred[64]{0:T(512)(128)(4,1)}, pred[64]{0:T(512)(128)(4,1)S(1)}, u32[]{:S(2)}) copy-start(pred[64]{0:T(512)(128)(4,1)S(1)} %compare_and_fusion.1) | copy-start | bytes 196
  32.6 58.7 %copy-start.12 = (s32[1024]{0:T(1024)}, s32[1024]{0:T(1024)S(1)}, u32[]{:S(2)}) copy-start(s32[1024]{0:T(1024)S(1)} %pad_clamp_fusion.1) | copy-start | bytes 12292
  33.2 11.7 %copy-start.19 = (s32[96]{0:T(128)S(1)}, s32[96]{0:T(128)}, u32[]{:S(2)}) copy-start(s32[96]{0:T(128)} %param.16) | copy-start | bytes 1156
  34.4 38.4 %all-to-all-start.1 = ((bf16[32,64,256]{2,0,1:T(8,128)(2,1)}), bf16[32,64,256]{2,0,1:T(8,128)(2,1)S(1)}, u32[]{:S(2)}, u32[]{:S(2)}) async-start(bf16[32,64,256]{2,0,1:T(8,128)(2,1)} %select_bitcast_fusion.3), calls=%async_computation.1 | async-start | bytes 2097152 | tf_op jit(solution)/shard_map/all_to_all | solution.py:61
  45.0 6.2 %copy-start.8 = (pred[16]{0:T(512)(128)(4,1)}, pred[16]{0:T(512)(128)(4,1)S(1)}, u32[]{:S(2)}) copy-start(pred[16]{0:T(512)(128)(4,1)S(1)} %get-tuple-element.6) | copy-start | bytes 52
  45.0 54.9 %copy-start.13 = (s32[1024]{0:T(1024)}, s32[1024]{0:T(1024)S(1)}, u32[]{:S(2)}) copy-start(s32[1024]{0:T(1024)S(1)} %pad_clamp_fusion.2) | copy-start | bytes 12292
  45.7 27.1 %copy-start.14 = (s32[1024]{0:T(1024)}, s32[1024]{0:T(1024)S(1)}, u32[]{:S(2)}) copy-start(s32[1024]{0:T(1024)S(1)} %pad_clamp_fusion) | copy-start | bytes 12292
  87.4 3.1 copy-start.5
  91.9 8.5 %copy-start.9 = (pred[16]{0:T(512)(128)(4,1)S(1)}, pred[16]{0:T(512)(128)(4,1)}, u32[]{:S(2)}) copy-start(pred[16]{0:T(512)(128)(4,1)} %copy-done.8) | copy-start | bytes 52
  93.1 34.7 %all-to-all-start.2 = ((bf16[32,64,256]{2,0,1:T(8,128)(2,1)}), bf16[32,64,256]{2,0,1:T(8,128)(2,1)S(1)}, u32[]{:S(2)}, u32[]{:S(2)}) async-start(bf16[32,64,256]{2,0,1:T(8,128)(2,1)} %select_bitcast_fusion.2), calls=%async_computation.2 | async-start | bytes 2097152 | tf_op jit(solution)/shard_map/all_to_all | solution.py:61
  142.4 3.1 copy-start.6
  145.5 1.6 copy-start.16
  147.1 8.8 %copy-start.10 = (pred[16]{0:T(512)(128)(4,1)S(1)}, pred[16]{0:T(512)(128)(4,1)}, u32[]{:S(2)}) copy-start(pred[16]{0:T(512)(128)(4,1)} %copy-done.8) | copy-start | bytes 52
  148.3 34.8 %all-to-all-start.3 = ((bf16[32,64,256]{2,0,1:T(8,128)(2,1)}), bf16[32,64,256]{2,0,1:T(8,128)(2,1)S(1)}, u32[]{:S(2)}, u32[]{:S(2)}) async-start(bf16[32,64,256]{2,0,1:T(8,128)(2,1)} %select_bitcast_fusion.1), calls=%async_computation.3 | async-start | bytes 2097152 | tf_op jit(solution)/shard_map/all_to_all | solution.py:61
  195.4 2.4 copy-start.3
  197.8 3.1 copy-start.7
  200.9 1.6 copy-start.17
  202.6 8.5 %copy-start.11 = (pred[16]{0:T(512)(128)(4,1)S(1)}, pred[16]{0:T(512)(128)(4,1)}, u32[]{:S(2)}) copy-start(pred[16]{0:T(512)(128)(4,1)} %copy-done.8) | copy-start | bytes 52
  203.7 34.5 %all-to-all-start.4 = ((bf16[32,64,256]{2,0,1:T(8,128)(2,1)}), bf16[32,64,256]{2,0,1:T(8,128)(2,1)S(1)}, u32[]{:S(2)}, u32[]{:S(2)}) async-start(bf16[32,64,256]{2,0,1:T(8,128)(2,1)} %select_bitcast_fusion), calls=%async_computation.4 | async-start | bytes 2097152 | tf_op jit(solution)/shard_map/all_to_all | solution.py:61
  210.2 70.3 %all-gather.2.cloned.1.call-start = ((), (), s32[]{:S(2)}) async-start(), calls=%async_computation.5 | async-start | bytes 1310720 | tf_op jit(solution)/shard_map/all_gather | solution.py:72
  250.5 2.4 copy-start.2
  252.9 3.1 copy-start.4
  257.6 195.4 %all-reduce.2.cloned.1.call-start = ((), (), s32[]{:S(2)}) async-start(), calls=%async_computation.6 | async-start | bytes 131072 | tf_op jit(solution)/shard_map/psum | solution.py:74
  280.5 197.7 %copy-start = (f32[128,2048]{1,0:T(8,128)S(1)}, f32[128,2048]{1,0:T(8,128)}, u32[]{:S(2)}) copy-start(f32[128,2048]{1,0:T(8,128)} %all-gather.2.cloned.1.call-done) | copy-start | bytes 3145732
Sparse Core Ops, SparseCore 0:
  257.7 22.6 all-gather.1
  283.9 169.0 all-reduce.1
where the time goes:
time: 492 us; the launch traced here: 487 us
  waiting for transfers between devices  277 us (56%)
  matrix products  108 us (22%)
  starting transfers between devices  44.4 us (9%)
  other arithmetic  31.9 us (6%)
  between operations  14.5 us (3%)
  local copies, waits for them, and re-layouts  11.2 us (2%)
    psum x1, waiting for transfers between devices, per_device(): gram = lax.psum(partial_gram, 'blk')  169 us
    all_to_all x4, waiting for transfers between devices, operate(): lax.all_to_all(packed, 'blk', split_axis=1, concat_axis=1, tiled=True)  85.2 us
    dot_general x8, matrix products, tile_products(): jnp.einsum('ctb,tab->cta', picked, real_part, preferred_element_type=jnp....  35.4 us
    dot_general x8, matrix products, tile_products(): jnp.einsum('ctb,tab->cta', picked, imag_part, preferred_element_type=jnp....  33.7 us
    all_to_all x4, starting transfers between devices, operate(): lax.all_to_all(packed, 'blk', split_axis=1, concat_axis=1, tiled=True)  30.8 us
    all_gather x1, waiting for transfers between devices, per_device(): gathered = lax.all_gather(current, 'col', axis=0, tiled=True)  22.6 us
    all_to_all x1, starting transfers between devices, per_device(): lax.all_to_all(fetch_row, 'blk', split_axis=0, concat_axis=0, tiled=True)  13.2 us
    another operation x3, other arithmetic, per_device(): lower = jnp.linalg.cholesky(gram)  12.4 us
  transfers between devices with their start and end apart: 7, of which 6 were waited for; matrix products, arithmetic and copies ran while one was open for 7% of the time, Pallas kernels for 0%

commit v1 on v0

--- a/solution.py
+++ b/solution.py
@@ -8,6 +8,19 @@
 STEPS = 4
 center = 1.25
 half_width = 0.75
+
+
+def collect(value, axis, dim):
+    ways = lax.axis_size(axis)
+    up = [(d, (d + 1) % ways) for d in range(ways)]
+    down = [(d, (d - 1) % ways) for d in range(ways)]
+    earlier, later = ([value], [value])
+    for _ in range(ways // 2):
+        earlier.append(lax.ppermute(earlier[-1], axis, up))
+    for _ in range((ways - 1) // 2):
+        later.append(lax.ppermute(later[-1], axis, down))
+    line = jnp.concatenate([*earlier[::-1], *later[1:]], axis=dim)
+    return jnp.roll(line, (lax.axis_index(axis) - ways // 2) * value.shape[dim], axis=dim)
 
 
 def turn(values):
@@ -69,7 +82,7 @@
     for step in range(1, STEPS):
         following = 2.0 * operate(current) - previous
         previous, current = (current, following)
-    gathered = lax.all_gather(current, "col", axis=0, tiled=True)
+    gathered = collect(current, "col", 0)
     partial_gram = jnp.dot(gathered, gathered.T, precision=lax.Precision.HIGHEST)
     gram = lax.psum(partial_gram, "blk")
     gram = gram + turn(turn(gram).T).T

time: 492 us -> 481 us (0.978)
  waiting for transfers between devices: 277 us -> 265 us
    all_gather x1 -> x0, waiting for transfers between devices: 22.6 us -> none  [per_device(): gathered = lax.all_gather(current, 'col', axis=0, tiled=True)]
    ppermute x0 -> x3, waiting for transfers between devices: none -> 9.97 us  [the longest x2 9.96 us: collect(): earlier.append(lax.ppermute(earlier[-1], axis, up))]
  transfers between devices with their start and end apart: 7 -> 9, of which waited for: 6 -> 7; matrix products, arithmetic and copies ran while one was open for 7% -> 8% of each run, Pallas kernels for 0% -> 0%
where the time goes in v1:
time: 481 us; the launch traced here: 476 us
  waiting for transfers between devices  265 us (55%)
  matrix products  106 us (22%)
  starting transfers between devices  48.4 us (10%)
  other arithmetic  31.3 us (7%)
  between operations  14.6 us (3%)
  local copies, waits for them, and re-layouts  10.6 us (2%)
    psum x1, waiting for transfers between devices, per_device(): gram = lax.psum(partial_gram, 'blk')  169 us
    all_to_all x4, waiting for transfers between devices, operate(): lax.all_to_all(packed, 'blk', split_axis=1, concat_axis=1, tiled=True)  85.5 us
    dot_general x8, matrix products, tile_products(): jnp.einsum('ctb,tab->cta', picked, real_part, preferred_element_type=jnp....  35.4 us
    dot_general x8, matrix products, tile_products(): jnp.einsum('ctb,tab->cta', picked, imag_part, preferred_element_type=jnp....  33.8 us
    all_to_all x4, starting transfers between devices, operate(): lax.all_to_all(packed, 'blk', split_axis=1, concat_axis=1, tiled=True)  30.8 us
    all_to_all x1, starting transfers between devices, per_device(): lax.all_to_all(fetch_row, 'blk', split_axis=0, concat_axis=0, tiled=True)  13.2 us
    another operation x3, other arithmetic, per_device(): lower = jnp.linalg.cholesky(gram)  12.4 us
    dot_general x8, matrix products, tile_products(): jnp.einsum('cta,tr->cra', prod_re, member, precision=lax.Precision.HIGHEST)  12.2 us
  transfers between devices with their start and end apart: 9, of which 7 were waited for; matrix products, arithmetic and copies ran while one was open for 8% of the time, Pallas kernels for 0%

profile of v1, /device:TPU:1, one launch (start us, length us, event | category | flops | bytes accessed | tf_op | source)
XLA Modules:
  0.0 475.9 jit_solution(3304380661674712893)
XLA Ops:
  6.5 1.4 copy.73
  7.9 13.2 %all-to-all-start = ((s32[64,1,1]{2,1,0:T(1,128)}), s32[64,1,1]{2,1,0:T(1,128)S(1)}, u32[]{:S(2)}, u32[]{:S(2)}) async-start(s32[64,1,1]{2,1,0:T(1,128)} %copy.73), calls=%async_computation | async-start | bytes 65536 | tf_op jit(solution)/shard_map/all_to_all | solution.py:67
  21.1 10.0 %fusion = f32[1,96,256]{2,0,1:T(1,128)S(1)} fusion(bf16[96,256,256]{2,1,0:T(8,128)(2,1)} %param.14, bf16[96,256,256]{2,1,0:T(8,128)(2,1)} %param.13), kind=kOutput, calls=%fused_computation.12 | convolution fusion | flops 31457280 | bytes 25264128 | tf_op jit(solution)/shard_map/tab,b->ta/dot_general | solution.py:49
  31.4 1.2 reduce.6
  32.6 0.6 gather_fusion.1
  33.2 1.2 select_bitcast_fusion.3
  34.4 10.6 %all-to-all-start.1 = ((bf16[32,64,256]{2,0,1:T(8,128)(2,1)}), bf16[32,64,256]{2,0,1:T(8,128)(2,1)S(1)}, u32[]{:S(2)}, u32[]{:S(2)}) async-start(bf16[32,64,256]{2,0,1:T(8,128)(2,1)} %select_bitcast_fusion.3), calls=%async_computation.1 | async-start | bytes 2097152 | tf_op jit(solution)/shard_map/all_to_all | solution.py:74
  45.7 2.3 fusion.96
  48.1 3.1 fusion.84
  51.2 21.7 %all-to-all-done.1 = bf16[32,64,256]{2,0,1:T(8,128)(2,1)S(1)} async-done(((bf16[32,64,256]{2,0,1:T(8,128)(2,1)}), bf16[32,64,256]{2,0,1:T(8,128)(2,1)S(1)}, u32[]{:S(2)}, u32[]{:S(2)}) %all-to-all-start.1) | async-done | bytes 1048608 | tf_op jit(solution)/shard_map/all_to_all | solution.py:74
  72.9 0.7 gather_fusion.2
  73.6 5.7 %fusion.48 = f32[32,80,256]{2,0,1:T(8,128)S(1)} fusion(bf16[96,256,256]{2,1,0:T(8,128)(2,1)} %param.14, bf16[80,32,256]{2,1,0:T(8,128)(2,1)S(1)} %gather_fusion.2, pred[80]{0:T(512)(128)(4,1)S(1)} %get-tuple-element.10), kind=kOutput, calls=%fused_computation.52 | convolution fusion | flops 336199680 | bytes 14418000 | tf_op jit(solution)/shard_map/ctb,tab->cta/dot_general | solution.py:33
  79.3 5.7 %fusion.36 = f32[32,80,256]{2,0,1:T(8,128)S(1)} fusion(bf16[96,256,256]{2,1,0:T(8,128)(2,1)} %param.13, bf16[80,32,256]{2,1,0:T(8,128)(2,1)S(1)} %gather_fusion.2, pred[80]{0:T(512)(128)(4,1)S(1)} %get-tuple-element.10), kind=kOutput, calls=%fused_computation.48 | convolution fusion | flops 336199680 | bytes 14418000 | tf_op jit(solution)/shard_map/ctb,tab->cta/dot_general | solution.py:32
  85.1 2.4 fusion.32
  88.1 2.4 fusion.34
  90.6 0.6 fusion.115
  91.4 0.6 gather_fusion.4
  92.0 1.2 select_bitcast_fusion.2
  93.2 7.0 %all-to-all-start.2 = ((bf16[32,64,256]{2,0,1:T(8,128)(2,1)}), bf16[32,64,256]{2,0,1:T(8,128)(2,1)S(1)}, u32[]{:S(2)}, u32[]{:S(2)}) async-start(bf16[32,64,256]{2,0,1:T(8,128)(2,1)} %select_bitcast_fusion.2), calls=%async_computation.2 | async-start | bytes 2097152 | tf_op jit(solution)/shard_map/all_to_all | solution.py:74
  100.7 2.3 fusion.99
  103.1 3.1 fusion.87
  106.2 21.8 %all-to-all-done.2 = bf16[32,64,256]{2,0,1:T(8,128)(2,1)S(1)} async-done(((bf16[32,64,256]{2,0,1:T(8,128)(2,1)}), bf16[32,64,256]{2,0,1:T(8,128)(2,1)S(1)}, u32[]{:S(2)}, u32[]{:S(2)}) %all-to-all-start.2) | async-done | bytes 1048608 | tf_op jit(solution)/shard_map/all_to_all | solution.py:74
  128.0 0.7 gather_fusion.5
  128.7 5.7 %fusion.51 = f32[32,80,256]{2,0,1:T(8,128)S(1)} fusion(bf16[96,256,256]{2,1,0:T(8,128)(2,1)} %param.14, bf16[80,32,256]{2,1,0:T(8,128)(2,1)S(1)} %gather_fusion.5, pred[80]{0:T(512)(128)(4,1)S(1)} %get-tuple-element.10), kind=kOutput, calls=%fused_computation.53 | convolution fusion | flops 336199680 | bytes 14418000 | tf_op jit(solution)/shard_map/ctb,tab->cta/dot_general | solution.py:33
  134.5 5.7 %fusion.39 = f32[32,80,256]{2,0,1:T(8,128)S(1)} fusion(bf16[96,256,256]{2,1,0:T(8,128)(2,1)} %param.13, bf16[80,32,256]{2,1,0:T(8,128)(2,1)S(1)} %gather_fusion.5, pred[80]{0:T(512)(128)(4,1)S(1)} %get-tuple-element.10), kind=kOutput, calls=%fused_computation.49 | convolution fusion | flops 336199680 | bytes 14418000 | tf_op jit(solution)/shard_map/ctb,tab->cta/dot_general | solution.py:32
  140.2 2.4 fusion.28
  143.3 2.4 fusion.30
  146.6 0.6 gather_fusion.7
  147.2 1.2 select_bitcast_fusion.1
  148.3 6.8 %all-to-all-start.3 = ((bf16[32,64,256]{2,0,1:T(8,128)(2,1)}), bf16[32,64,256]{2,0,1:T(8,128)(2,1)S(1)}, u32[]{:S(2)}, u32[]{:S(2)}) async-start(bf16[32,64,256]{2,0,1:T(8,128)(2,1)} %select_bitcast_fusion.1), calls=%async_computation.3 | async-start | bytes 2097152 | tf_op jit(solution)/shard_map/all_to_all | solution.py:74
  155.7 3.1 fusion.102
  158.8 3.1 fusion.90
  161.9 21.0 %all-to-all-done.3 = bf16[32,64,256]{2,0,1:T(8,128)(2,1)S(1)} async-done(((bf16[32,64,256]{2,0,1:T(8,128)(2,1)}), bf16[32,64,256]{2,0,1:T(8,128)(2,1)S(1)}, u32[]{:S(2)}, u32[]{:S(2)}) %all-to-all-start.3) | async-done | bytes 1048608 | tf_op jit(solution)/shard_map/all_to_all | solution.py:74
  183.0 0.7 gather_fusion.8
  183.7 5.7 %fusion.54 = f32[32,80,256]{2,0,1:T(8,128)S(1)} fusion(bf16[96,256,256]{2,1,0:T(8,128)(2,1)} %param.14, bf16[80,32,256]{2,1,0:T(8,128)(2,1)S(1)} %gather_fusion.8, pred[80]{0:T(512)(128)(4,1)S(1)} %get-tuple-element.10), kind=kOutput, calls=%fused_computation.54 | convolution fusion | flops 336199680 | bytes 14418000 | tf_op jit(solution)/shard_map/ctb,tab->cta/dot_general | solution.py:33
  189.4 5.7 %fusion.42 = f32[32,80,256]{2,0,1:T(8,128)S(1)} fusion(bf16[96,256,256]{2,1,0:T(8,128)(2,1)} %param.13, bf16[80,32,256]{2,1,0:T(8,128)(2,1)S(1)} %gather_fusion.8, pred[80]{0:T(512)(128)(4,1)S(1)} %get-tuple-element.10), kind=kOutput, calls=%fused_computation.50 | convolution fusion | flops 336199680 | bytes 14418000 | tf_op jit(solution)/shard_map/ctb,tab->cta/dot_general | solution.py:32
  195.1 2.4 fusion.24
  198.2 2.4 fusion.26
  201.6 0.6 gather_fusion.10
  202.2 1.2 select_bitcast_fusion
  203.4 6.5 %all-to-all-start.4 = ((bf16[32,64,256]{2,0,1:T(8,128)(2,1)}), bf16[32,64,256]{2,0,1:T(8,128)(2,1)S(1)}, u32[]{:S(2)}, u32[]{:S(2)}) async-start(bf16[32,64,256]{2,0,1:T(8,128)(2,1)} %select_bitcast_fusion), calls=%async_computation.4 | async-start | bytes 2097152 | tf_op jit(solution)/shard_map/all_to_all | solution.py:74
  210.7 3.1 fusion.105
  213.8 3.1 fusion.93
  216.9 20.9 %all-to-all-done.4 = bf16[32,64,256]{2,0,1:T(8,128)(2,1)S(1)} async-done(((bf16[32,64,256]{2,0,1:T(8,128)(2,1)}), bf16[32,64,256]{2,0,1:T(8,128)(2,1)S(1)}, u32[]{:S(2)}, u32[]{:S(2)}) %all-to-all-start.4) | async-done | bytes 1048608 | tf_op jit(solution)/shard_map/all_to_all | solution.py:74
  237.8 0.8 gather_fusion.11
  238.6 5.7 %fusion.57 = f32[32,80,256]{2,0,1:T(8,128)S(1)} fusion(bf16[96,256,256]{2,1,0:T(8,128)(2,1)} %param.14, bf16[80,32,256]{2,1,0:T(8,128)(2,1)S(1)} %gather_fusion.11, pred[80]{0:T(512)(128)(4,1)S(1)} %get-tuple-element.10), kind=kOutput, calls=%fused_computation.55 | convolution fusion | flops 336199680 | bytes 14418000 | tf_op jit(solution)/shard_map/ctb,tab->cta/dot_general | solution.py:33
  244.4 5.7 %fusion.45 = f32[32,80,256]{2,0,1:T(8,128)S(1)} fusion(bf16[96,256,256]{2,1,0:T(8,128)(2,1)} %param.13, bf16[80,32,256]{2,1,0:T(8,128)(2,1)S(1)} %gather_fusion.11, pred[80]{0:T(512)(128)(4,1)S(1)} %get-tuple-element.10), kind=kOutput, calls=%fused_computation.51 | convolution fusion | flops 336199680 | bytes 14418000 | tf_op jit(solution)/shard_map/ctb,tab->cta/dot_general | solution.py:32
  250.1 2.4 fusion.20
  253.2 2.4 fusion.22
  255.7 0.6 fusion.109
  256.6 1.3 collective-permute-start
  257.9 6.4 %collective-permute-done = f32[32,2048]{1,0:T(8,128)S(1)} collective-permute-done((f32[32,2048]{1,0:T(8,128)S(1)}, f32[32,2048]{1,0:T(8,128)S(1)}, u32[]{:S(2)}, u32[]{:S(2)}) %collective-permute-start) | collective-permute-done | bytes 262176 | tf_op jit(solution)/shard_map/ppermute | solution.py:19
  264.3 2.9 collective-permute-start.2
  267.2 3.5 collective-permute-done.1
  271.0 1.6 fusion.120
  272.6 169.1 %all-reduce.2.cloned.1.call-done = f32[128,128]{0,1:T(8,128)} async-done(((f32[128,128]{0,1:T(8,128)}), f32[128,128]{0,1:T(8,128)}) %all-reduce.2.cloned.1.call-update) | async-done | bytes 65552 | tf_op jit(solution)/shard_map/psum | solution.py:87
  441.7 0.9 copy.97
  443.0 0.9 add.133
  444.0 11.7 %cholesky.16 = f32[128,128]{1,0:T(8,128)S(1)} custom-call(f32[128,128]{1,0:T(8,128)S(1)} %fusion.142), custom_call_target="Cholesky" | custom-call | tf_op jit(solution)/shard_map/jit(cholesky)/cholesky | solution.py:89
  455.7 0.6 compare_reduce_fusion
  456.4 0.7 fusion.140
  457.0 9.8 %custom-call.7 = f32[1,128,128]{1,2,0:T(8,128)S(1)} custom-call(f32[1,128,128]{2,1,0:T(8,128)S(1)} %fusion.140), custom_call_target="InvertDiagBlocksLowerTriangular" | custom-call | tf_op jit(solution)/shard_map/jit(_solve_triangular)/triangular_solve | solution.py:90
  466.9 1.0 fusion.118
  467.9 0.7 dynamic-slice_multiply_fusion
  (82 shorter events, 8.1 us)
Async XLA Ops:
  7.9 23.5 %all-to-all-start = ((s32[64,1,1]{2,1,0:T(1,128)}), s32[64,1,1]{2,1,0:T(1,128)S(1)}, u32[]{:S(2)}, u32[]{:S(2)}) async-start(s32[64,1,1]{2,1,0:T(1,128)} %copy.73), calls=%async_computation | async-start | bytes 65536 | tf_op jit(solution)/shard_map/all_to_all | solution.py:67
  21.1 10.0 %copy-start.8 = (s32[96]{0:T(128)S(1)}, s32[96]{0:T(128)}, u32[]{:S(2)}) copy-start(s32[96]{0:T(128)} %param.15) | copy-start | bytes 1156
  21.1 10.2 %copy-start = (f32[32,2048]{1,0:T(8,128)S(1)}, f32[32,2048]{1,0:T(8,128)}, u32[]{:S(2)}) copy-start(f32[32,2048]{1,0:T(8,128)} %param.12) | copy-start | bytes 786436
  21.1 10.2 %copy-start.9 = (s32[96]{0:T(128)S(1)}, s32[96]{0:T(128)}, u32[]{:S(2)}) copy-start(s32[96]{0:T(128)} %param.16) | copy-start | bytes 1156
  34.4 38.5 %all-to-all-start.1 = ((bf16[32,64,256]{2,0,1:T(8,128)(2,1)}), bf16[32,64,256]{2,0,1:T(8,128)(2,1)S(1)}, u32[]{:S(2)}, u32[]{:S(2)}) async-start(bf16[32,64,256]{2,0,1:T(8,128)(2,1)} %select_bitcast_fusion.3), calls=%async_computation.1 | async-start | bytes 2097152 | tf_op jit(solution)/shard_map/all_to_all | solution.py:74
  45.1 137.8 %copy-start.7 = (s32[1024]{0:T(1024)}, s32[1024]{0:T(1024)S(1)}, u32[]{:S(2)}) copy-start(s32[1024]{0:T(1024)S(1)} %pad_clamp_fusion) | copy-start | bytes 12292
  87.5 3.1 copy-start.4
  93.2 34.8 %all-to-all-start.2 = ((bf16[32,64,256]{2,0,1:T(8,128)(2,1)}), bf16[32,64,256]{2,0,1:T(8,128)(2,1)S(1)}, u32[]{:S(2)}, u32[]{:S(2)}) async-start(bf16[32,64,256]{2,0,1:T(8,128)(2,1)} %select_bitcast_fusion.2), calls=%async_computation.2 | async-start | bytes 2097152 | tf_op jit(solution)/shard_map/all_to_all | solution.py:74
  142.6 3.1 copy-start.5
  148.3 34.6 %all-to-all-start.3 = ((bf16[32,64,256]{2,0,1:T(8,128)(2,1)}), bf16[32,64,256]{2,0,1:T(8,128)(2,1)S(1)}, u32[]{:S(2)}, u32[]{:S(2)}) async-start(bf16[32,64,256]{2,0,1:T(8,128)(2,1)} %select_bitcast_fusion.1), calls=%async_computation.3 | async-start | bytes 2097152 | tf_op jit(solution)/shard_map/all_to_all | solution.py:74
  195.1 2.4 copy-start.2
  197.6 3.1 copy-start.6
  203.4 34.5 %all-to-all-start.4 = ((bf16[32,64,256]{2,0,1:T(8,128)(2,1)}), bf16[32,64,256]{2,0,1:T(8,128)(2,1)S(1)}, u32[]{:S(2)}, u32[]{:S(2)}) async-start(bf16[32,64,256]{2,0,1:T(8,128)(2,1)} %select_bitcast_fusion), calls=%async_computation.4 | async-start | bytes 2097152 | tf_op jit(solution)/shard_map/all_to_all | solution.py:74
  209.8 231.9 %all-reduce.2.cloned.1.call-start = ((), (), s32[]{:S(2)}) async-start(), calls=%async_computation.5 | async-start | bytes 131072 | tf_op jit(solution)/shard_map/psum | solution.py:87
  250.1 2.4 copy-start.1
  252.6 3.1 copy-start.3
  256.6 7.7 %collective-permute-start = (f32[32,2048]{1,0:T(8,128)S(1)}, f32[32,2048]{1,0:T(8,128)S(1)}, u32[]{:S(2)}, u32[]{:S(2)}) collective-permute-start(f32[32,2048]{1,0:T(8,128)S(1)} %multiply_subtract_fusion), channel_id=1, source_target_pairs={{0,1},{1,2},{2,3},{3,0},{4,5},{5,6},{6,7},{7,4},{8,9},{9,10},{10,1... | collective-permute-start | bytes 786440 | tf_op jit(solution)/shard_map/ppermute | solution.py:19
  264.3 6.4 %collective-permute-start.1 = (f32[32,2048]{1,0:T(8,128)S(1)}, f32[32,2048]{1,0:T(8,128)S(1)}, u32[]{:S(2)}, u32[]{:S(2)}) collective-permute-start(f32[32,2048]{1,0:T(8,128)S(1)} %collective-permute-done), channel_id=1, source_target_pairs={{0,1},{1,2},{2,3},{3,0},{4,5},{5,6},{6,7},{7,4},{8,9},{9,10},{10,1... | collective-permute-start | bytes 786440 | tf_op jit(solution)/shard_map/ppermute | solution.py:19
  264.3 6.5 %collective-permute-start.2 = (f32[32,2048]{1,0:T(8,128)S(1)}, f32[32,2048]{1,0:T(8,128)S(1)}, u32[]{:S(2)}, u32[]{:S(2)}) collective-permute-start(f32[32,2048]{1,0:T(8,128)S(1)} %multiply_subtract_fusion), channel_id=1, source_target_pairs={{0,3},{1,0},{2,1},{3,2},{4,7},{5,4},{6,5},{7,6},{8,11},{9,8},{10,9... | collective-permute-start | bytes 786440 | tf_op jit(solution)/shard_map/ppermute | solution.py:21
Sparse Core Ops, SparseCore 0:
  272.7 168.9 all-reduce.1
